TPU v7x, 256 devices: a whole 4x4x8 slice. The times are simulated.
256 devices in a mesh: cp: 32 (over z, x_lo, core), tp: 8 (over y, x_hi).
Axes of the slice: x: 4 (x_hi: 2, x_lo: 2; x = x_hi * 2 + x_lo), y: 4, z: 8, core: 2. Of those that a mesh axis runs over, the one named last changes fastest.
Arguments:
- queries: bfloat16 [16384, 8192], P('cp', 'tp'), may hold values from -128 to 128
- keys: bfloat16 [16384, 1024], P(('cp', 'tp')), may hold values from -6 to 6
- values: bfloat16 [16384, 1024], P(('cp', 'tp')), may hold values from -6 to 6
- doc_ids: int32 [16384], P('cp'), may hold values from 0 to 31, never falling along the last dimension, each value on 1 to 4096 neighbouring positions
Outputs:
- attended: bfloat16 [16384, 8192], P('cp', 'tp')
Inputs may be any that keep to these rules, and one draw needn't show every extreme that they name: `doc_ids`: never falls along the positions; every document has 1 to 4096 positions and one has exactly 4096; every number from 0 to 31 is used.
All inputs are finite; a program needn't handle non-finite values.
Results may differ from a plain program's by a relative error of at most 0.0035.
Values may be sent and summed in bfloat16 or wider, within the bound.
No kernel may reach another device: no remote copies, remote signals or barrier semaphores. Data moves between devices by JAX's collectives and lax.ppermute only.
A program may use at most 64 MiB of HBM per device.

v0:
```python
import functools

import jax
import jax.numpy as jnp
from jax import lax
from jax.experimental import pallas as pl
from jax.experimental.pallas import tpu as pltpu
from jax.sharding import PartitionSpec as P

HEADS = 8
TP = 8
WIDTH = 128
BLOCK = 512
CHUNK = BLOCK // TP
TILE = 128
TILES = BLOCK // TILE
COLS = HEADS * TILE
ALL = TILES * COLS
AUG = WIDTH + 16
DOCS = BLOCK + 4 * WIDTH
PACK = DOCS + 16
SCALE = WIDTH**-0.5 * 1.4426950408889634
NEVER = -1e30
LIMIT = 2.0**100
f32, bf16 = jnp.float32, jnp.bfloat16
SPLIT_VMEM = 60
OWN_COST = (10**11, 1 << 20)
NEAR_COST = (10**4, 10**4)
NEXT_COST = (10**4, 10**4)
FAR_AFTER = 0
NEAR_AFTER = 0
VMEM = pl.BlockSpec(memory_space=pltpu.VMEM)
SMEM = pl.BlockSpec(memory_space=pltpu.SMEM)
ANY = pl.BlockSpec(memory_space=pl.ANY)
HBM = pl.BlockSpec(memory_space=pltpu.HBM)


def dot(a, b):
    return jnp.dot(a, b, preferred_element_type=f32)


def call(kernel, outs, operands, scratch=(), cost=(10**4, 10**4), vmem=32, specs=None, out_specs=None):
    return pl.pallas_call(
        kernel,
        out_shape=outs,
        in_specs=specs or [VMEM] * len(operands),
        out_specs=out_specs or jax.tree.map(lambda _: VMEM, outs),
        scratch_shapes=list(scratch),
        compiler_params=pltpu.CompilerParams(vmem_limit_bytes=vmem << 20),
        cost_estimate=pl.CostEstimate(flops=cost[0], bytes_accessed=cost[1], transcendentals=0),
    )(*operands)


def split_heads(k_hbm, v_hbm, out_ref, kv_ref, sems):
    copies = [pltpu.make_async_copy(ref, kv_ref.at[j], sems.at[j]) for j, ref in enumerate((k_hbm, v_hbm))]
    for copy in copies:
        copy.start()
    for copy in copies:
        copy.wait()
    for h in range(TP):
        for j in range(2):
            out_ref[h, j * CHUNK : (j + 1) * CHUNK] = kv_ref[j, :, h * WIDTH : (h + 1) * WIDTH]


def transpose_queries(q_hbm, qt_ref, q_ref, sem):
    copy = pltpu.make_async_copy(q_hbm, q_ref, sem)
    copy.start()
    copy.wait()
    for i in range(TILES):
        for h in range(HEADS):
            at = i * COLS + h * TILE
            qt_ref[:, at : at + TILE] = q_ref[i * TILE : (i + 1) * TILE, h * WIDTH : (h + 1) * WIDTH].T


def stack(count, *refs):
    out_ref = refs[-1]
    for j, block in enumerate(refs[:count]):
        out_ref[j] = block[...]


def pack_block(kv_ref, docs_ref, dep0_ref, dep1_ref, out_ref):
    del dep0_ref, dep1_ref
    for t in range(TP):
        out_ref[t * CHUNK : (t + 1) * CHUNK] = kv_ref[t, :CHUNK]
    for c in range(4):
        at = BLOCK + c * WIDTH
        v = jnp.concatenate([kv_ref[2 * c, CHUNK:], kv_ref[2 * c + 1, CHUNK:]], axis=0)
        out_ref[at : at + WIDTH] = v.T
    rows = [docs_ref[:, c * TILE : (c + 1) * TILE] for c in range(4)]
    out_ref[DOCS:] = jnp.concatenate([*rows, jnp.zeros((12, TILE), f32)], axis=0).astype(bf16)


def tiled(row):
    return jnp.concatenate([row] * HEADS, axis=1)


def own_mask(start_ref, i):
    count = (i + 1) * TILE
    u = lax.broadcasted_iota(jnp.int32, (count, TILE), 0)
    t = lax.broadcasted_iota(jnp.int32, (count, TILE), 1) + i * TILE
    allowed = (u <= t) & (u >= start_ref[:, i * TILE : (i + 1) * TILE])
    return jnp.concatenate([jnp.where(allowed, 0.0, NEVER)] * HEADS, axis=1)


def own_part(qt_ref, own_ref, docs_ref, start_ref, bias_ref, acc_ref, vt_ref):
    ones = jnp.ones((16, TILE), bf16)
    for c in range(4):
        at = BLOCK + c * WIDTH
        vt_ref[:WIDTH, c * TILE : (c + 1) * TILE] = own_ref[at : at + WIDTH]
        vt_ref[WIDTH:, c * TILE : (c + 1) * TILE] = ones
    first_doc = docs_ref[:, :1]
    for i in range(TILES):
        here = slice(i * TILE, (i + 1) * TILE)
        cols = slice(i * COLS, (i + 1) * COLS)
        count = (i + 1) * TILE
        scores = dot(own_ref[:count], qt_ref[:, cols]) * SCALE + own_mask(start_ref, i)
        bias = jnp.max(scores, axis=0, keepdims=True)
        weights = jnp.exp2(scores - bias).astype(bf16)
        acc_ref[:, cols] = dot(vt_ref[:, :count], weights)
        joins = tiled(jnp.broadcast_to(first_doc, (1, TILE)) == docs_ref[:, here])
        bias_ref[0:1, cols] = bias
        bias_ref[1:2, cols] = jnp.where(joins, bias, -NEVER)
        bias_ref[2:8, cols] = jnp.zeros((6, COLS), f32)


def gather_block(block_ref, at, doc, k_ref, vt_ref):
    count = jnp.zeros((1, TILE), f32)
    docs = block_ref[DOCS:].astype(f32)
    for c in range(4):
        at_v = BLOCK + c * WIDTH
        mask = jnp.where(docs[c : c + 1] == doc, 1.0, 0.0)
        mask16 = jnp.broadcast_to(mask, (16, TILE)).astype(bf16)
        lanes = pl.ds(at + (3 - c) * TILE, TILE)
        k_ref[lanes, :] = block_ref[c * TILE : (c + 1) * TILE]
        vt_ref[:WIDTH, lanes] = block_ref[at_v : at_v + WIDTH] * jnp.concatenate([mask16] * 8, axis=0)
        vt_ref[WIDTH:, lanes] = mask16
        count = count + mask
    return count


def add_keys(keys, tiles, qt_ref, bias_ref, k_ref, vt_ref, acc_in, put):
    def tile(i, _):
        cols = pl.ds(pl.multiple_of(i * COLS, COLS), COLS)
        qt, bias = qt_ref[:, cols], bias_ref[1:2, cols]
        weights = jnp.exp2(dot(k_ref[:keys], qt) * SCALE - bias).astype(bf16)
        put(i, acc_in[:, cols] + dot(vt_ref[:, :keys], weights))
        return 0

    lax.fori_loop(0, tiles, tile, 0)


def parity_places(core, base):
    mine = pl.multiple_of(base + (1 - core) * BLOCK, BLOCK)
    other = pl.multiple_of(base + core * BLOCK, BLOCK)
    return mine, other


def first_and_reach(docs_ref):
    docs = docs_ref[...]
    doc = docs[:, :1]
    rows = jnp.sum((docs == doc).astype(f32)).astype(jnp.int32)
    return doc, (rows + TILE - 1) // TILE


def steps_needed(count, step):
    keys = jnp.sum(count).astype(jnp.int32)
    return (keys + step - 1) // step


def add_gathered(count, most, step, tiles, qt_ref, bias_ref, k_ref, vt_ref, acc_in, put):
    need = steps_needed(count, step)
    for steps in range(1, most * BLOCK // step + 1):

        @pl.when(need == steps)
        def _(steps=steps):
            add_keys(steps * step, tiles, qt_ref, bias_ref, k_ref, vt_ref, acc_in, put)

    def tile(i, _):
        put(i, acc_in[:, pl.ds(pl.multiple_of(i * COLS, COLS), COLS)])
        return 0

    lax.fori_loop(jnp.where(need > 0, tiles, 0), TILES, tile, 0)


def putter(acc_out):
    def put(i, acc):
        acc_out[:, pl.ds(pl.multiple_of(i * COLS, COLS), COLS)] = acc

    return put


def gather_chips(core, doc, base, mine, theirs, first, k_ref, vt_ref):
    count = jnp.zeros((1, TILE), f32)
    for j in range(first, mine.shape[0]):
        x, y = parity_places(core, base)
        count += gather_block(mine.at[j], x, doc, k_ref, vt_ref)
        count += gather_block(theirs.at[j], y, doc, k_ref, vt_ref)
        base = base + 2 * BLOCK
    return count


def gather_near(core, doc, mine, theirs, k_ref, vt_ref):
    count = gather_block(theirs.at[0], 0, jnp.where(core == 1, doc, -jnp.ones_like(doc)), k_ref, vt_ref)
    return count + gather_chips(core, doc, core * BLOCK, mine, theirs, 1, k_ref, vt_ref)


def near_part(core_ref, docs_ref, qt_ref, bias_ref, acc_in, mine, theirs, acc_out, k_ref, vt_ref):
    doc, tiles = first_and_reach(docs_ref)
    count = gather_near(core_ref[0], doc, mine, theirs, k_ref, vt_ref)
    add_gathered(count, 3, 256, tiles, qt_ref, bias_ref, k_ref, vt_ref, acc_in, putter(acc_out))


def next_part(core_ref, docs_ref, qt_ref, bias_ref, acc_in, mine, theirs, acc_out, k_ref, vt_ref):
    doc, tiles = first_and_reach(docs_ref)
    x, y = parity_places(core_ref[0], 0)
    count = gather_block(mine, x, doc, k_ref, vt_ref) + gather_block(theirs, y, doc, k_ref, vt_ref)
    add_gathered(count, 2, 256, tiles, qt_ref, bias_ref, k_ref, vt_ref, acc_in, putter(acc_out))


def last_part(
    core_ref, docs_ref, start_ref, qt_ref, bias_ref, acc_in, own_ref, mine0, theirs0, mine1, theirs1, mine2, theirs2,
    out_ref, k_ref, vt_ref, acc_ref, flag_ref, done_ref, sems,
):
    core = core_ref[0]
    doc, tiles = first_and_reach(docs_ref)
    count = gather_chips(core, doc, 0, mine2, theirs2, 0, k_ref, vt_ref)

    def write(i):
        rows = pl.ds(pl.multiple_of(i * TILE, TILE), TILE)
        return pltpu.make_async_copy(done_ref.at[rows], out_ref.at[rows], sems.at[i])

    def finish(i, acc):
        total = acc[WIDTH : WIDTH + 1]
        flag_ref[1:2, pl.ds(pl.multiple_of(i * COLS, COLS), COLS)] = total
        final = (acc[:WIDTH] * (1.0 / total)).astype(bf16)
        rows = pl.ds(pl.multiple_of(i * TILE, TILE), TILE)
        for h in range(HEADS):
            done_ref[rows, h * WIDTH : (h + 1) * WIDTH] = final[:, h * TILE : (h + 1) * TILE].T
        write(i).start()

    add_gathered(count, 4, 256, tiles, qt_ref, bias_ref, k_ref, vt_ref, acc_in, finish)
    fine = jnp.min((flag_ref[1:2, :] < LIMIT).astype(f32))
    for i in range(TILES):
        write(i).wait()

    @pl.when(fine < 0.5)
    def _():
        pair_doc = jnp.where(core == 1, doc, -jnp.ones_like(doc))
        blocks = [(theirs0.at[0], pair_doc)]
        blocks += [(mine1, doc), (theirs1, doc)]
        for mine, theirs, first in ((mine0, theirs0, 1), (mine2, theirs2, 0)):
            for j in range(first, mine.shape[0]):
                blocks += [(mine.at[j], doc), (theirs.at[j], doc)]
        for i in range(TILES):
            cols = slice(i * COLS, (i + 1) * COLS)
            flag_ref[0:1, cols] = bias_ref[0:1, cols]
        first = first_acc(own_ref, start_ref, qt_ref, bias_ref, vt_ref)
        for i in range(TILES):
            acc_ref[:, i * COLS : (i + 1) * COLS] = first(i)
        for block_ref, block_doc in blocks:
            gather_block(block_ref, 0, block_doc, k_ref, vt_ref)
            mask = vt_ref[WIDTH : WIDTH + 1, :BLOCK].astype(f32)
            mask = jnp.concatenate(
                [jnp.broadcast_to(mask[:, c * TILE : (c + 1) * TILE], (TILE, TILE)).T for c in range(4)], axis=0
            )

            def tile(i, _, mask=mask):
                cols = pl.ds(pl.multiple_of(i * COLS, COLS), COLS)
                joins = bias_ref[1:2, cols] < 1e29
                allowed = (jnp.concatenate([mask] * HEADS, axis=1) > 0.5) & joins
                scores = jnp.where(allowed, dot(k_ref[:BLOCK], qt_ref[:, cols]), NEVER)
                old = flag_ref[0:1, cols]
                new = jnp.maximum(old, jnp.max(scores, axis=0, keepdims=True) * SCALE)
                weights = jnp.exp2(scores * SCALE - new).astype(bf16)
                acc_ref[:, cols] = acc_ref[:, cols] * jnp.exp2(old - new) + dot(vt_ref[:, :BLOCK], weights)
                flag_ref[0:1, cols] = new
                return 0

            lax.fori_loop(0, TILES, tile, 0)

        def last_tile(i, _):
            finish(i, acc_ref[:, pl.ds(pl.multiple_of(i * COLS, COLS), COLS)])
            write(i).wait()
            return 0

        lax.fori_loop(0, TILES, last_tile, 0)


def first_acc(own_ref, start_ref, qt_ref, bias_ref, vt_ref):
    for c in range(4):
        at = BLOCK + c * WIDTH
        vt_ref[:WIDTH, c * TILE : (c + 1) * TILE] = own_ref[at : at + WIDTH]
        vt_ref[WIDTH:, c * TILE : (c + 1) * TILE] = jnp.ones((16, TILE), bf16)

    def tile(i):
        cols = slice(i * COLS, (i + 1) * COLS)
        count = (i + 1) * TILE
        scores = dot(own_ref[:count], qt_ref[:, cols]) * SCALE + own_mask(start_ref, i)
        weights = jnp.exp2(scores - bias_ref[0:1, cols]).astype(bf16)
        return dot(vt_ref[:, :count], weights)

    return tile


def back(value, steps):
    count = lax.axis_size("cp")
    return lax.ppermute(value, "cp", [(s, s + steps) for s in range(count - steps)])


def other_core(value):
    return lax.ppermute(value, "cp", [(s, s ^ 1) for s in range(lax.axis_size("cp"))])


def per_device(queries, keys, values, doc_ids):
    shape = jax.ShapeDtypeStruct
    core = (lax.axis_index("cp") % 2).astype(jnp.int32).reshape(1)
    docs = (doc_ids + 1).astype(f32).reshape(1, BLOCK)
    start = jnp.sum(doc_ids[None, :] < doc_ids[:, None], axis=1).astype(jnp.int32).reshape(1, BLOCK)

    split = call(
        split_heads,
        shape((TP, 2 * CHUNK, WIDTH), bf16),
        (keys, values),
        [pltpu.VMEM((2, CHUNK, TP * WIDTH), bf16), pltpu.SemaphoreType.DMA((2,))],
        vmem=SPLIT_VMEM,
        specs=[HBM, HBM],
    )
    qt = call(
        transpose_queries,
        shape((WIDTH, ALL), bf16),
        (queries,),
        [pltpu.VMEM((BLOCK, HEADS * WIDTH), bf16), pltpu.SemaphoreType.DMA],
        specs=[HBM],
    )
    mine = lax.all_to_all(split, "tp", split_axis=0, concat_axis=0, tiled=True)
    packed = shape((PACK, WIDTH), bf16)
    own = call(pack_block, packed, (mine, docs, qt, start), specs=[VMEM, VMEM, ANY, ANY])

    def gathered(*blocks, after=()):
        count = len(blocks)
        outs = shape((count, PACK, WIDTH), bf16)
        specs = [VMEM] * count + [ANY] * len(after)
        mine = call(functools.partial(stack, count), outs, (*blocks, *after), specs=specs)
        return mine, other_core(mine)

    def scratch(blocks):
        return [pltpu.VMEM((blocks * BLOCK, WIDTH), bf16), pltpu.VMEM((AUG, blocks * BLOCK), bf16)]

    a4, a2 = back(own, 4), back(own, 2)
    a8, a6 = back(a4, 4), back(a4, 2)
    state = (shape((8, ALL), f32), shape((AUG, ALL), f32))
    operands = (qt, own, docs, start)
    bias, acc = call(own_part, state, operands, [pltpu.VMEM((AUG, BLOCK), bf16)], cost=OWN_COST)

    def add(part, acc, keys, blocks, cost):
        operands = (core, docs, qt, bias, acc, *keys)
        specs = [SMEM] + [VMEM] * 6
        return call(part, state[1], operands, scratch(blocks), cost=cost, specs=specs)

    near = gathered(own, a4, after=(bias,) if NEAR_AFTER else ())
    acc1 = add(near_part, acc, near, 4, NEAR_COST)
    mid = (a2, other_core(a2))
    acc = add(next_part, acc1, mid, 2, NEXT_COST)
    far = gathered(a6, a8, after=((acc1,), (acc,))[FAR_AFTER])
    return call(
        last_part,
        shape((BLOCK, HEADS * WIDTH), bf16),
        (core, docs, start, qt, bias, acc, own, *near, *mid, *far),
        [
            *scratch(4),
            pltpu.VMEM((AUG, ALL), f32),
            pltpu.VMEM((8, ALL), f32),
            pltpu.VMEM((BLOCK, HEADS * WIDTH), bf16),
            pltpu.SemaphoreType.DMA((TILES,)),
        ],
        cost=NEXT_COST,
        specs=[SMEM] + [VMEM] * 12,
        out_specs=HBM,
    )


def solution(mesh):
    placed = (P("cp", "tp"), P(("cp", "tp"), None), P(("cp", "tp"), None), P("cp"))
    return jax.shard_map(per_device, mesh=mesh, in_specs=placed, out_specs=P("cp", "tp"), check_vma=False)
```

profile of v0, /device:TPU:160, one launch (start us, length us, event | category | flops | bytes accessed | tf_op | source)
XLA Modules:
  0.0 59.2 jit_solution(1881841405140647417)
XLA Ops:
  0.0 0.0 copy-start.1
  0.0 1.7 %shard_map.47 = bf16[8,128,128]{2,1,0:T(8,128)(2,1)} custom-call(bf16[64,1024]{1,0:T(8,128)(2,1)} %k_hbm.1, bf16[64,1024]{1,0:T(8,128)(2,1)} %v_hbm.1), custom_call_target="tpu_custom_call" | custom-call | flops 10000 | bytes 10000 | tf_op jit(solution)/shard_map/pallas_call | solution.py:43
  1.8 6.9 %all-to-all-start = ((bf16[8,128,128]{2,1,0:T(8,128)(2,1)}), bf16[8,128,128]{2,1,0:T(8,128)(2,1)S(1)}, u32[]{:S(2)}, u32[]{:S(2)}) async-start(bf16[8,128,128]{2,1,0:T(8,128)(2,1)} %shard_map.47), calls=%async_computation | async-start | bytes 524288 | tf_op jit(solution)/shard_map/all_to_all | solution.py:335
  8.7 1.0 %convert_reduce_fusion = s32[512]{0:T(512)S(1)} fusion(s32[512]{0:T(512)} %param.7), kind=kLoop, calls=%fused_computation | loop fusion | flops 785920 | bytes 4096 | tf_op jit(solution)/shard_map/reduce_sum | solution.py:318
  9.7 0.0 copy-start
  9.7 1.2 %copy-done = bf16[512,1024]{1,0:T(8,128)(2,1)S(1)} copy-done((bf16[512,1024]{1,0:T(8,128)(2,1)S(1)}, bf16[512,1024]{1,0:T(8,128)(2,1)}, u32[]{:S(2)}) %copy-start) | copy-done | bytes 1048600
  10.9 0.4 shard_map.46.dep0_ref.qt_ref
  11.3 0.0 copy-done.1
  11.4 6.1 %all-to-all-done.kv_ref = bf16[8,128,128]{2,1,0:T(8,128)(2,1)S(1)} async-done(((bf16[8,128,128]{2,1,0:T(8,128)(2,1)}), bf16[8,128,128]{2,1,0:T(8,128)(2,1)S(1)}, u32[]{:S(2)}, u32[]{:S(2)}) %all-to-all-start) | async-done | bytes 262176 | tf_op jit(solution)/shard_map/all_to_all | solution.py:335
  17.5 0.1 shard_map.48.own_ref.refs_0_
  17.6 2.9 %collective-permute-start = (bf16[1040,128]{1,0:T(8,128)(2,1)S(1)}, bf16[1040,128]{1,0:T(8,128)(2,1)S(1)}, u32[]{:S(2)}, u32[]{:S(2)}) collective-permute-start(bf16[1040,128]{1,0:T(8,128)(2,1)S(1)} %shard_map.48.own_ref.refs_0_), channel_id=1, source_target_pairs={{0,32},{8,40},{16,48},{24,56},{32,64},{40,72},{48,80},{56,88},{64,... | collective-permute-start | bytes 798728 | tf_op jit(solution)/shard_map/ppermute | solution.py:307
  20.5 2.5 %collective-permute-start.2 = (bf16[1040,128]{1,0:T(8,128)(2,1)S(1)}, bf16[1040,128]{1,0:T(8,128)(2,1)S(1)}, u32[]{:S(2)}, u32[]{:S(2)}) collective-permute-start(bf16[1040,128]{1,0:T(8,128)(2,1)S(1)} %shard_map.48.own_ref.refs_0_), channel_id=1, source_target_pairs={{0,16},{8,24},{16,32},{24,40},{32,48},{40,56},{48,64},{56,72},{64,... | collective-permute-start | bytes 798728 | tf_op jit(solution)/shard_map/ppermute | solution.py:307
  23.0 3.1 %collective-permute-done.refs_1_ = bf16[1040,128]{1,0:T(8,128)(2,1)S(1)} collective-permute-done((bf16[1040,128]{1,0:T(8,128)(2,1)S(1)}, bf16[1040,128]{1,0:T(8,128)(2,1)S(1)}, u32[]{:S(2)}, u32[]{:S(2)}) %collective-permute-start) | collective-permute-done | bytes 266272 | tf_op jit(solution)/shard_map/ppermute | solution.py:307
  26.2 0.1 collective-permute-start.1
  26.3 2.9 %collective-permute-start.5 = (bf16[1040,128]{1,0:T(8,128)(2,1)S(1)}, bf16[1040,128]{1,0:T(8,128)(2,1)S(1)}, u32[]{:S(2)}, u32[]{:S(2)}) collective-permute-start(bf16[1040,128]{1,0:T(8,128)(2,1)S(1)} %collective-permute-done.refs_1_), channel_id=1, source_target_pairs={{0,32},{8,40},{16,48},{24,56},{32,64},{40,72},{48,80},{56,88},{64,... | collective-permute-start | bytes 798728 | tf_op jit(solution)/shard_map/ppermute | solution.py:307
  29.3 4.7 %collective-permute-start.4 = (bf16[1040,128]{1,0:T(8,128)(2,1)S(1)}, bf16[1040,128]{1,0:T(8,128)(2,1)S(1)}, u32[]{:S(2)}, u32[]{:S(2)}) collective-permute-start(bf16[1040,128]{1,0:T(8,128)(2,1)S(1)} %collective-permute-done.refs_1_), channel_id=1, source_target_pairs={{0,16},{8,24},{16,32},{24,40},{32,48},{40,56},{48,64},{56,72},{64,... | collective-permute-start | bytes 798728 | tf_op jit(solution)/shard_map/ppermute | solution.py:307
  33.9 2.3 %shard_map.49 = (f32[8,4096]{1,0:T(8,128)S(1)}, f32[144,4096]{1,0:T(8,128)S(1)}) custom-call(bf16[128,4096]{1,0:T(8,128)(2,1)S(1)} %shard_map.46.dep0_ref.qt_ref, bf16[1040,128]{1,0:T(8,128)(2,1)S(1)} %shard_map.48.own_ref.refs_0_, f32[1,512]{1,0:T(1,128)S(1)} %bitcast.4, s32[1,512]{1,0:T(1,128)S(1)} %bitcast.9), custom_call_target="tpu_custom_call" | custom-call | flops 99999997952 | bytes 1048576 | tf_op jit(solution)/shard_map/pallas_call | solution.py:43
  36.3 0.0 collective-permute-done.1.theirs.theirs0
  36.3 4.5 %shard_map.51.acc_in.refs_2_ = f32[144,4096]{1,0:T(8,128)S(1)} custom-call(s32[1]{0:T(128)} %bitcast.core_ref, f32[1,512]{1,0:T(1,128)S(1)} %bitcast.5, bf16[128,4096]{1,0:T(8,128)(2,1)S(1)} %shard_map.46.dep0_ref.qt_ref, f32[8,4096]{1,0:T(8,128)S(1)} %get-tuple-element.7.bias_ref, f32[144,4096]{1,0:T(8,128)S(1)} %get-tuple-element.8.acc_in, ...), custom_call_target="tpu_custom_call" | custom-call | flops 10000 | bytes 10000 | tf_op jit(solution)/shard_map/pallas_call | solution.py:43
  40.7 0.0 collective-permute-done.5.refs_1_
  40.7 4.6 %collective-permute-done.4.refs_0_ = bf16[1040,128]{1,0:T(8,128)(2,1)S(1)} collective-permute-done((bf16[1040,128]{1,0:T(8,128)(2,1)S(1)}, bf16[1040,128]{1,0:T(8,128)(2,1)S(1)}, u32[]{:S(2)}, u32[]{:S(2)}) %collective-permute-start.4) | collective-permute-done | bytes 266272 | tf_op jit(solution)/shard_map/ppermute | solution.py:307
  45.4 0.1 collective-permute-start.6
  45.5 0.0 collective-permute-done.2.mine.mine1
  45.5 0.5 collective-permute-start.3
  46.0 1.8 %collective-permute-done.3.theirs.theirs1 = bf16[1040,128]{1,0:T(8,128)(2,1)S(1)} collective-permute-done((bf16[1040,128]{1,0:T(8,128)(2,1)S(1)}, bf16[1040,128]{1,0:T(8,128)(2,1)S(1)}, u32[]{:S(2)}, u32[]{:S(2)}) %collective-permute-start.3) | collective-permute-done | bytes 266272 | tf_op jit(solution)/shard_map/ppermute | solution.py:311
  47.8 4.6 %shard_map.52.acc_in = f32[144,4096]{1,0:T(8,128)S(1)} custom-call(s32[1]{0:T(128)} %bitcast.core_ref, f32[1,512]{1,0:T(1,128)S(1)} %bitcast.6, bf16[128,4096]{1,0:T(8,128)(2,1)S(1)} %shard_map.46.dep0_ref.qt_ref, f32[8,4096]{1,0:T(8,128)S(1)} %get-tuple-element.7.bias_ref, f32[144,4096]{1,0:T(8,128)S(1)} %shard_map.51.acc_in.refs_2_, ...), custom_call_target="tpu_custom_call" | custom-call | flops 10000 | bytes 10000 | tf_op jit(solution)/shard_map/pallas_call | solution.py:43
  52.4 0.0 collective-permute-done.6.theirs2
  52.4 6.7 %shard_map.54 = bf16[512,1024]{1,0:T(8,128)(2,1)} custom-call(s32[1]{0:T(128)} %bitcast.core_ref, f32[1,512]{1,0:T(1,128)S(1)} %bitcast.7, s32[1,512]{1,0:T(1,128)S(1)} %bitcast.10, bf16[128,4096]{1,0:T(8,128)(2,1)S(1)} %shard_map.46.dep0_ref.qt_ref, f32[8,4096]{1,0:T(8,128)S(1)} %get-tuple-element.7.bias_ref, f32[144,4096]{1,0:T(8,128)S(1)} %shard_map.52.acc_in, ...), custom_call_target="tpu_custom_call" | custom-call | flops 10000 | bytes 10000 | tf_op jit(solution)/shard_map/pallas_call | solution.py:43
  (3 shorter events, 0.1 us)
Async XLA Ops:
  0.0 11.3 %copy-start.1 = (s32[512]{0:T(512)S(1)}, s32[512]{0:T(512)}, u32[]{:S(2)}) copy-start(s32[512]{0:T(512)} %param.7) | copy-start | bytes 6148
  1.8 15.7 %all-to-all-start = ((bf16[8,128,128]{2,1,0:T(8,128)(2,1)}), bf16[8,128,128]{2,1,0:T(8,128)(2,1)S(1)}, u32[]{:S(2)}, u32[]{:S(2)}) async-start(bf16[8,128,128]{2,1,0:T(8,128)(2,1)} %shard_map.47), calls=%async_computation | async-start | bytes 524288 | tf_op jit(solution)/shard_map/all_to_all | solution.py:335
  9.7 1.2 %copy-start = (bf16[512,1024]{1,0:T(8,128)(2,1)S(1)}, bf16[512,1024]{1,0:T(8,128)(2,1)}, u32[]{:S(2)}) copy-start(bf16[512,1024]{1,0:T(8,128)(2,1)} %q_hbm.1) | copy-start | bytes 3145732
  17.6 8.6 %collective-permute-start = (bf16[1040,128]{1,0:T(8,128)(2,1)S(1)}, bf16[1040,128]{1,0:T(8,128)(2,1)S(1)}, u32[]{:S(2)}, u32[]{:S(2)}) collective-permute-start(bf16[1040,128]{1,0:T(8,128)(2,1)S(1)} %shard_map.48.own_ref.refs_0_), channel_id=1, source_target_pairs={{0,32},{8,40},{16,48},{24,56},{32,64},{40,72},{48,80},{56,88},{64,... | collective-permute-start | bytes 798728 | tf_op jit(solution)/shard_map/ppermute | solution.py:307
  20.5 25.0 %collective-permute-start.2 = (bf16[1040,128]{1,0:T(8,128)(2,1)S(1)}, bf16[1040,128]{1,0:T(8,128)(2,1)S(1)}, u32[]{:S(2)}, u32[]{:S(2)}) collective-permute-start(bf16[1040,128]{1,0:T(8,128)(2,1)S(1)} %shard_map.48.own_ref.refs_0_), channel_id=1, source_target_pairs={{0,16},{8,24},{16,32},{24,40},{32,48},{40,56},{48,64},{56,72},{64,... | collective-permute-start | bytes 798728 | tf_op jit(solution)/shard_map/ppermute | solution.py:307
  26.2 10.0 %collective-permute-start.1 = (bf16[2,1040,128]{2,1,0:T(8,128)(2,1)S(1)}, bf16[2,1040,128]{2,1,0:T(8,128)(2,1)S(1)}, u32[]{:S(2)}, u32[]{:S(2)}) collective-permute-start(bf16[2,1040,128]{2,1,0:T(8,128)(2,1)S(1)} %shard_map.50.mine.mine0), channel_id=1, source_target_pairs={{0,8},{8,0},{16,24},{24,16},{32,40},{40,32},{48,56},{56,48},{64,72... | collective-permute-start | bytes 1597448 | tf_op jit(solution)/shard_map/ppermute | solution.py:311
  26.3 14.4 %collective-permute-start.5 = (bf16[1040,128]{1,0:T(8,128)(2,1)S(1)}, bf16[1040,128]{1,0:T(8,128)(2,1)S(1)}, u32[]{:S(2)}, u32[]{:S(2)}) collective-permute-start(bf16[1040,128]{1,0:T(8,128)(2,1)S(1)} %collective-permute-done.refs_1_), channel_id=1, source_target_pairs={{0,32},{8,40},{16,48},{24,56},{32,64},{40,72},{48,80},{56,88},{64,... | collective-permute-start | bytes 798728 | tf_op jit(solution)/shard_map/ppermute | solution.py:307
  29.3 16.1 %collective-permute-start.4 = (bf16[1040,128]{1,0:T(8,128)(2,1)S(1)}, bf16[1040,128]{1,0:T(8,128)(2,1)S(1)}, u32[]{:S(2)}, u32[]{:S(2)}) collective-permute-start(bf16[1040,128]{1,0:T(8,128)(2,1)S(1)} %collective-permute-done.refs_1_), channel_id=1, source_target_pairs={{0,16},{8,24},{16,32},{24,40},{32,48},{40,56},{48,64},{56,72},{64,... | collective-permute-start | bytes 798728 | tf_op jit(solution)/shard_map/ppermute | solution.py:307
  45.4 7.0 %collective-permute-start.6 = (bf16[2,1040,128]{2,1,0:T(8,128)(2,1)S(1)}, bf16[2,1040,128]{2,1,0:T(8,128)(2,1)S(1)}, u32[]{:S(2)}, u32[]{:S(2)}) collective-permute-start(bf16[2,1040,128]{2,1,0:T(8,128)(2,1)S(1)} %shard_map.53.mine2), channel_id=1, source_target_pairs={{0,8},{8,0},{16,24},{24,16},{32,40},{40,32},{48,56},{56,48},{64,72... | collective-permute-start | bytes 1597448 | tf_op jit(solution)/shard_map/ppermute | solution.py:311
  45.5 2.3 %collective-permute-start.3 = (bf16[1040,128]{1,0:T(8,128)(2,1)S(1)}, bf16[1040,128]{1,0:T(8,128)(2,1)S(1)}, u32[]{:S(2)}, u32[]{:S(2)}) collective-permute-start(bf16[1040,128]{1,0:T(8,128)(2,1)S(1)} %collective-permute-done.2.mine.mine1), channel_id=1, source_target_pairs={{0,8},{8,0},{16,24},{24,16},{32,40},{40,32},{48,56},{56,48},{64,72... | collective-permute-start | bytes 798728 | tf_op jit(solution)/shard_map/ppermute | solution.py:311
where the time goes:
time: 58.4 us; the launch traced here: 59.2 us
  starting transfers between devices  20.6 us (35%)
  Pallas kernels  20.3 us (35%)
  waiting for transfers between devices  15.7 us (27%)
  local copies, waits for them, and re-layouts  1.23 us (2%)
  other arithmetic  1.01 us (2%)
    pallas_call x9, Pallas kernels, call(): pl.pallas_call(kernel, out_shape=outs, in_specs=specs or [VMEM] * len(ope...  20.3 us
    ppermute x4, starting transfers between devices, back(): lax.ppermute(value, 'cp', [(s, s + steps) for s in range(count - steps)])  13 us
    ppermute x4, waiting for transfers between devices, back(): lax.ppermute(value, 'cp', [(s, s + steps) for s in range(count - steps)])  7.8 us
    all_to_all x1, starting transfers between devices, per_device(): mine = lax.all_to_all(split, 'tp', split_axis=0, concat_axis=0, tiled=True)  6.94 us
    all_to_all x1, waiting for transfers between devices, per_device(): mine = lax.all_to_all(split, 'tp', split_axis=0, concat_axis=0, tiled=True)  6.12 us
    ppermute x3, waiting for transfers between devices, other_core(): lax.ppermute(value, 'cp', [(s, s ^ 1) for s in range(lax.axis_size('cp'))])  1.79 us
    unnamed x4, local copies, waits for them, and re-layouts  1.23 us
  transfers between devices with their start and end apart: 8, of which 4 were waited for; matrix products, arithmetic and copies ran while one was open for 2% of the time, Pallas kernels for 20%

commit v1 on v0

--- a/solution.py
+++ b/solution.py
@@ -189,9 +189,9 @@
     return put
 
 
-def gather_chips(core, doc, base, mine, theirs, first, k_ref, vt_ref):
+def gather_chips(core, doc, base, mine, theirs, order, k_ref, vt_ref):
     count = jnp.zeros((1, TILE), f32)
-    for j in range(first, mine.shape[0]):
+    for j in order:
         x, y = parity_places(core, base)
         count += gather_block(mine.at[j], x, doc, k_ref, vt_ref)
         count += gather_block(theirs.at[j], y, doc, k_ref, vt_ref)
@@ -201,7 +201,7 @@
 
 def gather_near(core, doc, mine, theirs, k_ref, vt_ref):
     count = gather_block(theirs.at[0], 0, jnp.where(core == 1, doc, -jnp.ones_like(doc)), k_ref, vt_ref)
-    return count + gather_chips(core, doc, core * BLOCK, mine, theirs, 1, k_ref, vt_ref)
+    return count + gather_chips(core, doc, core * BLOCK, mine, theirs, (1,), k_ref, vt_ref)
 
 
 def near_part(core_ref, docs_ref, qt_ref, bias_ref, acc_in, mine, theirs, acc_out, k_ref, vt_ref):
@@ -223,7 +223,7 @@
 ):
     core = core_ref[0]
     doc, tiles = first_and_reach(docs_ref)
-    count = gather_chips(core, doc, 0, mine2, theirs2, 0, k_ref, vt_ref)
+    count = gather_chips(core, doc, 0, mine2, theirs2, (1, 0), k_ref, vt_ref)
 
     def write(i):
         rows = pl.ds(pl.multiple_of(i * TILE, TILE), TILE)
@@ -347,7 +347,7 @@
         return [pltpu.VMEM((blocks * BLOCK, WIDTH), bf16), pltpu.VMEM((AUG, blocks * BLOCK), bf16)]
 
     a4, a2 = back(own, 4), back(own, 2)
-    a8, a6 = back(a4, 4), back(a4, 2)
+    a6, a8 = back(a4, 2), back(a4, 4)
     state = (shape((8, ALL), f32), shape((AUG, ALL), f32))
     operands = (qt, own, docs, start)
     bias, acc = call(own_part, state, operands, [pltpu.VMEM((AUG, BLOCK), bf16)], cost=OWN_COST)
@@ -361,7 +361,7 @@
     acc1 = add(near_part, acc, near, 4, NEAR_COST)
     mid = (a2, other_core(a2))
     acc = add(next_part, acc1, mid, 2, NEXT_COST)
-    far = gathered(a6, a8, after=((acc1,), (acc,))[FAR_AFTER])
+    far = gathered(a8, a6, after=((acc1,), (acc,))[FAR_AFTER])
     return call(
         last_part,
         shape((BLOCK, HEADS * WIDTH), bf16),

time: 58.4 us -> 56.9 us (0.974)
  the two profiles are of different devices: /device:TPU:160 before, /device:TPU:66 now
where the time goes in v1:
time: 56.9 us; the launch traced here: 56.5 us
  starting transfers between devices  27.6 us (49%)
  Pallas kernels  18.3 us (32%)
  waiting for transfers between devices  7.99 us (14%)
  local copies, waits for them, and re-layouts  1.23 us (2%)
  other arithmetic  1.01 us (2%)
    ppermute x4, starting transfers between devices, back(): lax.ppermute(value, 'cp', [(s, s + steps) for s in range(count - steps)])  19.5 us
    pallas_call x9, Pallas kernels, call(): pl.pallas_call(kernel, out_shape=outs, in_specs=specs or [VMEM] * len(ope...  18.3 us
    all_to_all x1, waiting for transfers between devices, per_device(): mine = lax.all_to_all(split, 'tp', split_axis=0, concat_axis=0, tiled=True)  6.12 us
    all_to_all x1, starting transfers between devices, per_device(): mine = lax.all_to_all(split, 'tp', split_axis=0, concat_axis=0, tiled=True)  6.04 us
    ppermute x3, starting transfers between devices, other_core(): lax.ppermute(value, 'cp', [(s, s ^ 1) for s in range(lax.axis_size('cp'))])  2.04 us
    ppermute x3, waiting for transfers between devices, other_core(): lax.ppermute(value, 'cp', [(s, s ^ 1) for s in range(lax.axis_size('cp'))])  1.82 us
    unnamed x4, local copies, waits for them, and re-layouts  1.23 us
  transfers between devices with their start and end apart: 8, of which 2 were waited for; matrix products, arithmetic and copies ran while one was open for 2% of the time, Pallas kernels for 21%

profile of v1, /device:TPU:66, one launch (start us, length us, event | category | flops | bytes accessed | tf_op | source)
XLA Modules:
  0.0 56.5 jit_solution(12880875480339391388)
XLA Ops:
  0.0 0.0 copy-start.1
  0.0 1.7 %shard_map.47 = bf16[8,128,128]{2,1,0:T(8,128)(2,1)} custom-call(bf16[64,1024]{1,0:T(8,128)(2,1)} %k_hbm.1, bf16[64,1024]{1,0:T(8,128)(2,1)} %v_hbm.1), custom_call_target="tpu_custom_call" | custom-call | flops 10000 | bytes 10000 | tf_op jit(solution)/shard_map/pallas_call | solution.py:43
  1.8 6.0 %all-to-all-start = ((bf16[8,128,128]{2,1,0:T(8,128)(2,1)}), bf16[8,128,128]{2,1,0:T(8,128)(2,1)S(1)}, u32[]{:S(2)}, u32[]{:S(2)}) async-start(bf16[8,128,128]{2,1,0:T(8,128)(2,1)} %shard_map.47), calls=%async_computation | async-start | bytes 524288 | tf_op jit(solution)/shard_map/all_to_all | solution.py:335
  7.8 1.0 %convert_reduce_fusion = s32[512]{0:T(512)S(1)} fusion(s32[512]{0:T(512)} %param.7), kind=kLoop, calls=%fused_computation | loop fusion | flops 785920 | bytes 4096 | tf_op jit(solution)/shard_map/reduce_sum | solution.py:318
  8.8 0.0 copy-start
  8.8 1.2 %copy-done = bf16[512,1024]{1,0:T(8,128)(2,1)S(1)} copy-done((bf16[512,1024]{1,0:T(8,128)(2,1)S(1)}, bf16[512,1024]{1,0:T(8,128)(2,1)}, u32[]{:S(2)}) %copy-start) | copy-done | bytes 1048600
  10.0 0.4 shard_map.46.dep0_ref.qt_ref
  10.4 0.0 copy-done.1
  10.5 6.1 %all-to-all-done.kv_ref = bf16[8,128,128]{2,1,0:T(8,128)(2,1)S(1)} async-done(((bf16[8,128,128]{2,1,0:T(8,128)(2,1)}), bf16[8,128,128]{2,1,0:T(8,128)(2,1)S(1)}, u32[]{:S(2)}, u32[]{:S(2)}) %all-to-all-start) | async-done | bytes 262176 | tf_op jit(solution)/shard_map/all_to_all | solution.py:335
  16.6 0.1 shard_map.48.own_ref.refs_0_
  16.7 3.8 %collective-permute-start = (bf16[1040,128]{1,0:T(8,128)(2,1)S(1)}, bf16[1040,128]{1,0:T(8,128)(2,1)S(1)}, u32[]{:S(2)}, u32[]{:S(2)}) collective-permute-start(bf16[1040,128]{1,0:T(8,128)(2,1)S(1)} %shard_map.48.own_ref.refs_0_), channel_id=1, source_target_pairs={{0,32},{8,40},{16,48},{24,56},{32,64},{40,72},{48,80},{56,88},{64,... | collective-permute-start | bytes 798728 | tf_op jit(solution)/shard_map/ppermute | solution.py:307
  20.5 5.9 %collective-permute-start.2 = (bf16[1040,128]{1,0:T(8,128)(2,1)S(1)}, bf16[1040,128]{1,0:T(8,128)(2,1)S(1)}, u32[]{:S(2)}, u32[]{:S(2)}) collective-permute-start(bf16[1040,128]{1,0:T(8,128)(2,1)S(1)} %shard_map.48.own_ref.refs_0_), channel_id=1, source_target_pairs={{0,16},{8,24},{16,32},{24,40},{32,48},{40,56},{48,64},{56,72},{64,... | collective-permute-start | bytes 798728 | tf_op jit(solution)/shard_map/ppermute | solution.py:307
  26.4 0.0 collective-permute-done.refs_1_
  26.5 0.1 collective-permute-start.1
  26.6 4.1 %collective-permute-start.5 = (bf16[1040,128]{1,0:T(8,128)(2,1)S(1)}, bf16[1040,128]{1,0:T(8,128)(2,1)S(1)}, u32[]{:S(2)}, u32[]{:S(2)}) collective-permute-start(bf16[1040,128]{1,0:T(8,128)(2,1)S(1)} %collective-permute-done.refs_1_), channel_id=1, source_target_pairs={{0,16},{8,24},{16,32},{24,40},{32,48},{40,56},{48,64},{56,72},{64,... | collective-permute-start | bytes 798728 | tf_op jit(solution)/shard_map/ppermute | solution.py:307
  30.8 5.6 %collective-permute-start.4 = (bf16[1040,128]{1,0:T(8,128)(2,1)S(1)}, bf16[1040,128]{1,0:T(8,128)(2,1)S(1)}, u32[]{:S(2)}, u32[]{:S(2)}) collective-permute-start(bf16[1040,128]{1,0:T(8,128)(2,1)S(1)} %collective-permute-done.refs_1_), channel_id=1, source_target_pairs={{0,32},{8,40},{16,48},{24,56},{32,64},{40,72},{48,80},{56,88},{64,... | collective-permute-start | bytes 798728 | tf_op jit(solution)/shard_map/ppermute | solution.py:307
  36.4 2.3 %shard_map.49 = (f32[8,4096]{1,0:T(8,128)S(1)}, f32[144,4096]{1,0:T(8,128)S(1)}) custom-call(bf16[128,4096]{1,0:T(8,128)(2,1)S(1)} %shard_map.46.dep0_ref.qt_ref, bf16[1040,128]{1,0:T(8,128)(2,1)S(1)} %shard_map.48.own_ref.refs_0_, f32[1,512]{1,0:T(1,128)S(1)} %bitcast.4, s32[1,512]{1,0:T(1,128)S(1)} %bitcast.9), custom_call_target="tpu_custom_call" | custom-call | flops 99999997952 | bytes 1048576 | tf_op jit(solution)/shard_map/pallas_call | solution.py:43
  38.7 0.0 collective-permute-done.1.theirs.theirs0
  38.7 4.4 %shard_map.51.acc_in.refs_2_ = f32[144,4096]{1,0:T(8,128)S(1)} custom-call(s32[1]{0:T(128)} %bitcast.core_ref, f32[1,512]{1,0:T(1,128)S(1)} %bitcast.5, bf16[128,4096]{1,0:T(8,128)(2,1)S(1)} %shard_map.46.dep0_ref.qt_ref, f32[8,4096]{1,0:T(8,128)S(1)} %get-tuple-element.7.bias_ref, f32[144,4096]{1,0:T(8,128)S(1)} %get-tuple-element.8.acc_in, ...), custom_call_target="tpu_custom_call" | custom-call | flops 10000 | bytes 10000 | tf_op jit(solution)/shard_map/pallas_call | solution.py:43
  43.2 0.0 collective-permute-done.5.refs_1_
  43.2 0.0 collective-permute-done.4.refs_0_
  43.2 1.8 %collective-permute-start.6 = (bf16[2,1040,128]{2,1,0:T(8,128)(2,1)S(1)}, bf16[2,1040,128]{2,1,0:T(8,128)(2,1)S(1)}, u32[]{:S(2)}, u32[]{:S(2)}) collective-permute-start(bf16[2,1040,128]{2,1,0:T(8,128)(2,1)S(1)} %shard_map.53.mine2), channel_id=1, source_target_pairs={{0,8},{8,0},{16,24},{24,16},{32,40},{40,32},{48,56},{56,48},{64,72... | collective-permute-start | bytes 1597448 | tf_op jit(solution)/shard_map/ppermute | solution.py:311
  45.1 0.0 collective-permute-done.2.mine.mine1
  45.1 0.1 collective-permute-start.3
  45.2 1.8 %collective-permute-done.3.theirs.theirs1 = bf16[1040,128]{1,0:T(8,128)(2,1)S(1)} collective-permute-done((bf16[1040,128]{1,0:T(8,128)(2,1)S(1)}, bf16[1040,128]{1,0:T(8,128)(2,1)S(1)}, u32[]{:S(2)}, u32[]{:S(2)}) %collective-permute-start.3) | collective-permute-done | bytes 266272 | tf_op jit(solution)/shard_map/ppermute | solution.py:311
  47.0 4.6 %shard_map.52.acc_in = f32[144,4096]{1,0:T(8,128)S(1)} custom-call(s32[1]{0:T(128)} %bitcast.core_ref, f32[1,512]{1,0:T(1,128)S(1)} %bitcast.6, bf16[128,4096]{1,0:T(8,128)(2,1)S(1)} %shard_map.46.dep0_ref.qt_ref, f32[8,4096]{1,0:T(8,128)S(1)} %get-tuple-element.7.bias_ref, f32[144,4096]{1,0:T(8,128)S(1)} %shard_map.51.acc_in.refs_2_, ...), custom_call_target="tpu_custom_call" | custom-call | flops 10000 | bytes 10000 | tf_op jit(solution)/shard_map/pallas_call | solution.py:43
  51.6 0.0 collective-permute-done.6.theirs2
  51.6 4.7 %shard_map.54 = bf16[512,1024]{1,0:T(8,128)(2,1)} custom-call(s32[1]{0:T(128)} %bitcast.core_ref, f32[1,512]{1,0:T(1,128)S(1)} %bitcast.7, s32[1,512]{1,0:T(1,128)S(1)} %bitcast.10, bf16[128,4096]{1,0:T(8,128)(2,1)S(1)} %shard_map.46.dep0_ref.qt_ref, f32[8,4096]{1,0:T(8,128)S(1)} %get-tuple-element.7.bias_ref, f32[144,4096]{1,0:T(8,128)S(1)} %shard_map.52.acc_in, ...), custom_call_target="tpu_custom_call" | custom-call | flops 10000 | bytes 10000 | tf_op jit(solution)/shard_map/pallas_call | solution.py:43
  (3 shorter events, 0.1 us)
Async XLA Ops:
  0.0 10.4 %copy-start.1 = (s32[512]{0:T(512)S(1)}, s32[512]{0:T(512)}, u32[]{:S(2)}) copy-start(s32[512]{0:T(512)} %param.7) | copy-start | bytes 6148
  1.8 14.8 %all-to-all-start = ((bf16[8,128,128]{2,1,0:T(8,128)(2,1)}), bf16[8,128,128]{2,1,0:T(8,128)(2,1)S(1)}, u32[]{:S(2)}, u32[]{:S(2)}) async-start(bf16[8,128,128]{2,1,0:T(8,128)(2,1)} %shard_map.47), calls=%async_computation | async-start | bytes 524288 | tf_op jit(solution)/shard_map/all_to_all | solution.py:335
  8.8 1.2 %copy-start = (bf16[512,1024]{1,0:T(8,128)(2,1)S(1)}, bf16[512,1024]{1,0:T(8,128)(2,1)}, u32[]{:S(2)}) copy-start(bf16[512,1024]{1,0:T(8,128)(2,1)} %q_hbm.1) | copy-start | bytes 3145732
  16.7 9.8 %collective-permute-start = (bf16[1040,128]{1,0:T(8,128)(2,1)S(1)}, bf16[1040,128]{1,0:T(8,128)(2,1)S(1)}, u32[]{:S(2)}, u32[]{:S(2)}) collective-permute-start(bf16[1040,128]{1,0:T(8,128)(2,1)S(1)} %shard_map.48.own_ref.refs_0_), channel_id=1, source_target_pairs={{0,32},{8,40},{16,48},{24,56},{32,64},{40,72},{48,80},{56,88},{64,... | collective-permute-start | bytes 798728 | tf_op jit(solution)/shard_map/ppermute | solution.py:307
  20.5 24.5 %collective-permute-start.2 = (bf16[1040,128]{1,0:T(8,128)(2,1)S(1)}, bf16[1040,128]{1,0:T(8,128)(2,1)S(1)}, u32[]{:S(2)}, u32[]{:S(2)}) collective-permute-start(bf16[1040,128]{1,0:T(8,128)(2,1)S(1)} %shard_map.48.own_ref.refs_0_), channel_id=1, source_target_pairs={{0,16},{8,24},{16,32},{24,40},{32,48},{40,56},{48,64},{56,72},{64,... | collective-permute-start | bytes 798728 | tf_op jit(solution)/shard_map/ppermute | solution.py:307
  26.5 12.2 %collective-permute-start.1 = (bf16[2,1040,128]{2,1,0:T(8,128)(2,1)S(1)}, bf16[2,1040,128]{2,1,0:T(8,128)(2,1)S(1)}, u32[]{:S(2)}, u32[]{:S(2)}) collective-permute-start(bf16[2,1040,128]{2,1,0:T(8,128)(2,1)S(1)} %shard_map.50.mine.mine0), channel_id=1, source_target_pairs={{0,8},{8,0},{16,24},{24,16},{32,40},{40,32},{48,56},{56,48},{64,72... | collective-permute-start | bytes 1597448 | tf_op jit(solution)/shard_map/ppermute | solution.py:311
  26.6 16.5 %collective-permute-start.5 = (bf16[1040,128]{1,0:T(8,128)(2,1)S(1)}, bf16[1040,128]{1,0:T(8,128)(2,1)S(1)}, u32[]{:S(2)}, u32[]{:S(2)}) collective-permute-start(bf16[1040,128]{1,0:T(8,128)(2,1)S(1)} %collective-permute-done.refs_1_), channel_id=1, source_target_pairs={{0,16},{8,24},{16,32},{24,40},{32,48},{40,56},{48,64},{56,72},{64,... | collective-permute-start | bytes 798728 | tf_op jit(solution)/shard_map/ppermute | solution.py:307
  30.8 12.4 %collective-permute-start.4 = (bf16[1040,128]{1,0:T(8,128)(2,1)S(1)}, bf16[1040,128]{1,0:T(8,128)(2,1)S(1)}, u32[]{:S(2)}, u32[]{:S(2)}) collective-permute-start(bf16[1040,128]{1,0:T(8,128)(2,1)S(1)} %collective-permute-done.refs_1_), channel_id=1, source_target_pairs={{0,32},{8,40},{16,48},{24,56},{32,64},{40,72},{48,80},{56,88},{64,... | collective-permute-start | bytes 798728 | tf_op jit(solution)/shard_map/ppermute | solution.py:307
  43.2 8.3 %collective-permute-start.6 = (bf16[2,1040,128]{2,1,0:T(8,128)(2,1)S(1)}, bf16[2,1040,128]{2,1,0:T(8,128)(2,1)S(1)}, u32[]{:S(2)}, u32[]{:S(2)}) collective-permute-start(bf16[2,1040,128]{2,1,0:T(8,128)(2,1)S(1)} %shard_map.53.mine2), channel_id=1, source_target_pairs={{0,8},{8,0},{16,24},{24,16},{32,40},{40,32},{48,56},{56,48},{64,72... | collective-permute-start | bytes 1597448 | tf_op jit(solution)/shard_map/ppermute | solution.py:311
  45.1 1.9 %collective-permute-start.3 = (bf16[1040,128]{1,0:T(8,128)(2,1)S(1)}, bf16[1040,128]{1,0:T(8,128)(2,1)S(1)}, u32[]{:S(2)}, u32[]{:S(2)}) collective-permute-start(bf16[1040,128]{1,0:T(8,128)(2,1)S(1)} %collective-permute-done.2.mine.mine1), channel_id=1, source_target_pairs={{0,8},{8,0},{16,24},{24,16},{32,40},{40,32},{48,56},{56,48},{64,72... | collective-permute-start | bytes 798728 | tf_op jit(solution)/shard_map/ppermute | solution.py:311
